TPU v7x, 32 devices: a whole 2x2x4 slice. The times are simulated.
32 devices in a mesh: lat: 16 (over z, x, core), lev: 2 (over y).
Axes of the slice: x: 2, y: 2, z: 4, core: 2. Of those that a mesh axis runs over, the one named last changes fastest.
Arguments:
- zonal_wind: float32 [8, 256, 2880], P('lev', 'lat'), may hold values from -6 to 6
- merid_wind: float32 [8, 256, 2880], P('lev', 'lat'), may hold values from -6 to 6
- tracer: float32 [8, 256, 2880], P('lev', 'lat'), may hold values from -6 to 6
- vertical_wind: float32 [8, 256, 2880], P('lev', 'lat'), may hold values from -6 to 6
- cutoff: int32 [256], replicated, may hold values from 1 to 1440, as said below
Outputs:
- zonal_next: float32 [8, 256, 2880], P('lev', 'lat')
- merid_next: float32 [8, 256, 2880], P('lev', 'lat')
- tracer_next: float32 [8, 256, 2880], P('lev', 'lat')
Inputs may be any that keep to these rules, and one draw needn't show every extreme that they name: With d the distance of latitude j in rows from the nearer pole (d = 1 for the first and last latitude): cutoff is 1 at d = 1, 719 at d = 40, between 1 and 719 for d < 40, and 1440 for d > 40.
All inputs are finite; a program needn't handle non-finite values.
Results may differ from a plain program's by a relative error of at most 0.0001.
Values sent between devices are 32-bit elements; how exact they have to be, the bound alone decides.
A program may use at most 128 MiB of HBM per device.

v0:
```python
import math

import jax
import jax.numpy as jnp
import ml_dtypes
import numpy as np
from jax import lax
from jax.experimental import pallas as pl
from jax.experimental.pallas import tpu as pltpu
from jax.sharding import PartitionSpec as P

NLON = 2880
KMAX = 720
HALF = NLON // 2
CHUNK = 128
MESH = pl.DeviceIdType.MESH
QUARTER = 0.025


def half_tables():
    modes = KMAX // 2
    chunks = -(-modes // CHUNK)
    tables = np.zeros((2, chunks, HALF, 2 * CHUNK), np.float32)
    points = np.arange(HALF, dtype=np.int64)
    for parity in range(2):
        for chunk in range(chunks):
            ids = np.arange(chunk * CHUNK, min((chunk + 1) * CHUNK, modes), dtype=np.int64)
            angles = (points[:, None] * (2 * ids + parity)[None, :] % NLON) * (2.0 * math.pi / NLON)
            tables[parity, chunk, :, : len(ids)] = np.cos(angles)
            tables[parity, chunk, :, CHUNK : CHUNK + len(ids)] = np.sin(angles)
    tables = tables.reshape(2 * chunks, HALF, 2 * CHUNK)
    high = tables.astype(ml_dtypes.bfloat16)
    low = (tables - high.astype(np.float32)).astype(ml_dtypes.bfloat16)
    return high, low


def split(x):
    high = x.astype(jnp.bfloat16)
    return high, (x - high.astype(jnp.float32)).astype(jnp.bfloat16)


def dot(a, b, transposed=False):
    dims = (((1,), (1 if transposed else 0,)), ((), ()))
    return lax.dot_general(a, b, dims, preferred_element_type=jnp.float32)


def filter_kernel(chunks, flag_ref, zonal, merid, tracer, cut_ref, high_ref, low_ref, out_ref, xh, xl, acc):
    step = pl.program_id(0)
    steps = 2 * chunks
    parity = step // chunks
    chunk = step % chunks
    fields = (zonal, merid, tracer)
    levels, lat_rows = zonal.shape[0], zonal.shape[1]
    rows = levels * lat_rows
    active = flag_ref[0] > 0

    @pl.when(jnp.logical_and(step == 0, jnp.logical_not(active)))
    def _():
        for f in range(3):
            out_ref[f] = fields[f][...]

    @pl.when(jnp.logical_and(step == 0, active))
    def _():
        for f in range(3):
            for l in range(levels):
                x = fields[f][l]
                first, second = x[:, :HALF], x[:, HALF:]
                at = pl.ds(f * rows + l * lat_rows, lat_rows)
                for p, folded in enumerate((first + second, first - second)):
                    high, low = split(folded)
                    xh[p, at, :] = high
                    xl[p, at, :] = low

    @pl.when(active)
    def _():
        th, tl = high_ref[0], low_ref[0]
        spectrum = dot(xh[parity], th) + dot(xl[parity], th) + dot(xh[parity], tl)
        lane = lax.broadcasted_iota(jnp.int32, spectrum.shape, 1) % CHUNK
        mode = 2 * (chunk * CHUNK + lane) + parity
        factor = jnp.where(mode == 0, jnp.float32(1.0 / NLON), jnp.float32(2.0 / NLON))
        spectrum = jnp.where(mode <= cut_ref[...], spectrum * factor, 0.0)
        sh, sl = split(spectrum)
        part = dot(sh, th, True) + dot(sl, th, True) + dot(sh, tl, True)

        @pl.when(chunk == 0)
        def _():
            acc[parity] = part

        @pl.when(chunk > 0)
        def _():
            acc[parity] += part

    @pl.when(jnp.logical_and(step == steps - 1, active))
    def _():
        for f in range(3):
            for l in range(levels):
                at = pl.ds(f * rows + l * lat_rows, lat_rows)
                keep = cut_ref[at, :] < HALF
                even, odd = acc[0, at, :], acc[1, at, :]
                y = jnp.concatenate([even + odd, even - odd], axis=1)
                out_ref[f, l] = jnp.where(keep, y, fields[f][l])


def filtered_fields(zonal, merid, tracer, own_cut):
    high, low = half_tables()
    steps = high.shape[0]
    levels, lat_rows, _ = zonal.shape
    rows = 3 * levels * lat_rows
    flag = jnp.any(own_cut < HALF).astype(jnp.int32)[None]
    cuts = jnp.tile(own_cut, 3 * levels)[:, None]
    whole = pl.BlockSpec((levels, lat_rows, NLON), lambda i, flag: (0, 0, 0))
    table = pl.BlockSpec((1, HALF, 2 * CHUNK), lambda i, flag: (i * flag[0], 0, 0))
    return pl.pallas_call(
        lambda *refs: filter_kernel(steps // 2, *refs),
        out_shape=jax.ShapeDtypeStruct((3, levels, lat_rows, NLON), jnp.float32),
        grid_spec=pltpu.PrefetchScalarGridSpec(
            num_scalar_prefetch=1,
            grid=(steps,),
            in_specs=[whole, whole, whole, pl.BlockSpec((rows, 1), lambda i, flag: (0, 0)), table, table],
            out_specs=pl.BlockSpec((3, levels, lat_rows, NLON), lambda i, flag: (0, 0, 0, 0)),
            scratch_shapes=[
                pltpu.VMEM((2, rows, HALF), jnp.bfloat16),
                pltpu.VMEM((2, rows, HALF), jnp.bfloat16),
                pltpu.VMEM((2, rows, HALF), jnp.float32),
            ],
        ),
        compiler_params=pltpu.CompilerParams(vmem_limit_bytes=40 * 1024 * 1024),
    )(flag, zonal, merid, tracer, cuts, jnp.asarray(high), jnp.asarray(low))


def latitude_factors(total_rows):
    ids = np.arange(total_rows + 1, dtype=np.float64)
    face = np.sin(ids * (math.pi / total_rows))
    center = np.sin((ids[:-1] + 0.5) * (math.pi / total_rows))
    return np.stack(
        [QUARTER * face[:-1] / center, QUARTER * face[1:] / center, QUARTER / center], axis=1
    ).astype(np.float32)


def east_of(x):
    return jnp.concatenate([x[:, 1:], x[:, :1]], axis=1)


def west_of(x):
    return jnp.concatenate([x[:, -1:], x[:, :-1]], axis=1)


def advect_kernel(
    lat_count, lev_count, field_ref, wind_ref, factor_ref,
    out0, out1, out2, lev_field, lev_wind, lat_out, lat_in, send_sem, recv_sem,
):
    lat, lev = lax.axis_index("lat"), lax.axis_index("lev")
    outs = (out0, out1, out2)
    levels, lat_rows = wind_ref.shape[0], wind_ref.shape[1]
    has = (lev > 0, lev < lev_count - 1, lat > 0, lat < lat_count - 1)
    there = ((lat, lev - 1), (lat, lev + 1), (lat - 1, lev), (lat + 1, lev))

    barrier = pltpu.get_barrier_semaphore()
    for side in range(4):
        @pl.when(has[side])
        def _():
            pl.semaphore_signal(barrier, inc=1, device_id=there[side], device_id_type=MESH)

    for f in range(3):
        for l in range(levels):
            lat_out[0, f * levels + l : f * levels + l + 1, :] = field_ref[f, l, 0:1, :]
            lat_out[1, f * levels + l : f * levels + l + 1, :] = field_ref[f, l, lat_rows - 1 : lat_rows, :]
    pl.semaphore_wait(barrier, sum(side.astype(jnp.int32) for side in has))

    def remote(slot, source, target, to):
        return pltpu.make_async_remote_copy(
            src_ref=source, dst_ref=target, send_sem=send_sem.at[slot], recv_sem=recv_sem.at[slot],
            device_id=there[to], device_id_type=MESH,
        )

    lats = (
        (remote(4, lat_out.at[1], lat_in.at[0], 3), 3, 2),
        (remote(5, lat_out.at[0], lat_in.at[1], 2), 2, 3),
    )
    levs = (
        (remote(2, wind_ref.at[levels - 1], lev_wind.at[0], 1), 1, 0),
        (remote(3, wind_ref.at[0], lev_wind.at[1], 0), 0, 1),
        (remote(0, field_ref.at[:, levels - 1], lev_field.at[0], 1), 1, 0),
        (remote(1, field_ref.at[:, 0], lev_field.at[1], 0), 0, 1),
    )
    for copy, to, _ in lats + levs:
        pl.when(has[to])(copy.start)

    for side in range(2):
        @pl.when(jnp.logical_not(has[side]))
        def _():
            lev_field[side] = jnp.zeros(lev_field.shape[1:], jnp.float32)
            lev_wind[side] = jnp.zeros(lev_wind.shape[1:], jnp.float32)

        @pl.when(jnp.logical_not(has[2 + side]))
        def _():
            lat_in[side] = jnp.zeros(lat_in.shape[1:], jnp.float32)

    factors = factor_ref[pl.ds(pl.multiple_of(lat * lat_rows, lat_rows), lat_rows), :]
    row = lax.broadcasted_iota(jnp.int32, (lat_rows, 1), 0)
    low_face = jnp.where(row > 0, factors[:, 0:1], 0.0)
    high_face = jnp.where(row < lat_rows - 1, factors[:, 1:2], 0.0)
    zonal_factor = factors[:, 2:3]

    def inner(l, carry):
        below, above = jnp.maximum(l - 1, 0), jnp.minimum(l + 1, levels - 1)
        zonal = field_ref[0, l]
        merid = field_ref[1, l]
        wind_here = wind_ref[l]
        east_wind = (zonal + east_of(zonal)) * zonal_factor
        merid_pair = merid + jnp.roll(merid, 1, axis=0)
        low_wind = jnp.where(l > 0, jnp.float32(QUARTER), 0.0) * (wind_ref[below] + wind_here)
        high_wind = jnp.where(l < levels - 1, jnp.float32(QUARTER), 0.0) * (wind_here + wind_ref[above])
        for f in range(3):
            x = field_ref[f, l]
            flux_x = east_wind * (x + east_of(x))
            flux_y = merid_pair * (x + jnp.roll(x, 1, axis=0))
            div_y = high_face * jnp.roll(flux_y, -1, axis=0) - low_face * flux_y
            div_z = high_wind * (x + field_ref[f, above]) - low_wind * (field_ref[f, below] + x)
            outs[f][l] = x - (flux_x - west_of(flux_x)) - div_y - div_z
        return carry

    lax.fori_loop(0, levels, inner, 0)

    for copy, to, source in lats:
        pl.when(has[source])(copy.wait_recv)
    for side, at, factor in ((0, 0, factors[0:1, 0:1]), (1, lat_rows - 1, -factors[lat_rows - 1 :, 1:2])):
        for l in range(levels):
            own = pl.ds(at, 1)
            pair = factor * (lat_in[side, levels + l : levels + l + 1, :] + field_ref[1, l, own, :])
            for f in range(3):
                halo = lat_in[side, f * levels + l : f * levels + l + 1, :]
                outs[f][l, own, :] += pair * (halo + field_ref[f, l, own, :])

    for copy, to, source in levs:
        pl.when(has[source])(copy.wait_recv)
    for side, l, sign in ((0, 0, QUARTER), (1, levels - 1, -QUARTER)):
        pair = sign * (lev_wind[side] + wind_ref[l])
        for f in range(3):
            outs[f][l] += pair * (lev_field[side, f] + field_ref[f, l])
    for copy, to, _ in lats + levs:
        pl.when(has[to])(copy.wait_send)


def advected(fields, wind, lat_count, lev_count):
    levels, lat_rows, _ = wind.shape
    vmem = pl.BlockSpec(memory_space=pltpu.VMEM)
    one = jax.ShapeDtypeStruct(wind.shape, jnp.float32)
    return pl.pallas_call(
        lambda *refs: advect_kernel(lat_count, lev_count, *refs),
        out_shape=(one, one, one),
        in_specs=[vmem] * 3,
        out_specs=(vmem,) * 3,
        scratch_shapes=[
            pltpu.VMEM((2, 3, lat_rows, NLON), jnp.float32),
            pltpu.VMEM((2, lat_rows, NLON), jnp.float32),
            pltpu.VMEM((2, 3 * levels, NLON), jnp.float32),
            pltpu.VMEM((2, 3 * levels, NLON), jnp.float32),
            pltpu.SemaphoreType.DMA((6,)),
            pltpu.SemaphoreType.DMA((6,)),
        ],
        compiler_params=pltpu.CompilerParams(
            collective_id=0, has_side_effects=True, vmem_limit_bytes=32 * 1024 * 1024
        ),
    )(fields, wind, jnp.asarray(latitude_factors(lat_rows * lat_count)))


def solution(mesh):
    lat_count, lev_count = mesh.shape["lat"], mesh.shape["lev"]

    def on_device(zonal_wind, merid_wind, tracer, vertical_wind, cutoff):
        lat_rows = zonal_wind.shape[1]
        own_cut = lax.dynamic_slice_in_dim(cutoff, lax.axis_index("lat") * lat_rows, lat_rows)
        fields = filtered_fields(zonal_wind, merid_wind, tracer, own_cut)
        return advected(fields, vertical_wind, lat_count, lev_count)

    spec = P("lev", "lat", None)
    return jax.shard_map(
        on_device, mesh=mesh, in_specs=(spec,) * 4 + (P(),), out_specs=(spec,) * 3, check_vma=False
    )
```

profile of v0, /device:TPU:1, one launch (start us, length us, event | category | flops | bytes accessed | tf_op | source)
XLA Modules:
  0.0 48.9 jit_solution(7215360066021523140)
XLA Ops:
  0.6 1.4 %compare_reduce_fusion = (pred[]{:T(512)}, s32[16]{0:T(128)S(1)}) fusion(s32[256]{0:T(256)} %param.12, s32[]{:T(128)S(6)} %select_n.3), kind=kLoop, calls=%fused_computation | loop fusion | flops 31 | bytes 133 | tf_op jit(solution)/shard_map/reduce_or | solution.py:109
  2.7 0.1 broadcast_in_dim_tile.4.refs_4_
  2.8 0.0 copy-start
  2.8 2.2 %copy-done = bf16[6,1440,256]{2,1,0:T(8,128)(2,1)S(1)} copy-done((bf16[6,1440,256]{2,1,0:T(8,128)(2,1)S(1)}, bf16[6,1440,256]{2,1,0:T(8,128)(2,1)}, u32[]{:S(2)}) %copy-start) | copy-done | bytes 4423704
  5.1 0.0 copy-start.1
  5.1 2.3 %copy-done.1 = bf16[6,1440,256]{2,1,0:T(8,128)(2,1)S(1)} copy-done((bf16[6,1440,256]{2,1,0:T(8,128)(2,1)S(1)}, bf16[6,1440,256]{2,1,0:T(8,128)(2,1)}, u32[]{:S(2)}) %copy-start.1) | copy-done | bytes 4423704
  7.3 0.0 copy-start.3
  7.3 1.1 %copy-done.3 = f32[4,16,2880]{2,1,0:T(8,128)S(1)} copy-done((f32[4,16,2880]{2,1,0:T(8,128)S(1)}, f32[4,16,2880]{2,1,0:T(8,128)}, u32[]{:S(2)}) %copy-start.3) | copy-done | bytes 737304
  8.4 0.0 copy-start.4
  8.4 1.1 %copy-done.4 = f32[4,16,2880]{2,1,0:T(8,128)S(1)} copy-done((f32[4,16,2880]{2,1,0:T(8,128)S(1)}, f32[4,16,2880]{2,1,0:T(8,128)}, u32[]{:S(2)}) %copy-start.4) | copy-done | bytes 737304
  9.5 0.0 copy-start.5
  9.6 1.1 %copy-done.5 = f32[4,16,2880]{2,1,0:T(8,128)S(1)} copy-done((f32[4,16,2880]{2,1,0:T(8,128)S(1)}, f32[4,16,2880]{2,1,0:T(8,128)}, u32[]{:S(2)}) %copy-start.5) | copy-done | bytes 737304
  10.7 0.0 copy-start.2
  10.7 0.0 copy-start.6
  10.7 15.0 %shard_map.103.refs_0_ = f32[3,4,16,2880]{3,2,1,0:T(8,128)S(1)} custom-call(s32[1]{0:T(128)} %bitcast.refs_0_, f32[4,16,2880]{2,1,0:T(8,128)S(1)} %copy-done.3, f32[4,16,2880]{2,1,0:T(8,128)S(1)} %copy-done.4, f32[4,16,2880]{2,1,0:T(8,128)S(1)} %copy-done.5, s32[192,1]{1,0:T(8,128)S(1)} %broadcast_in_dim_tile.4.refs_4_, bf16[6,1440,256]{2,1,0:T(8,128)(2,1)S(1)} %copy-done.1, ...), custom_call_target="tpu_custom_call" | custom-call | tf_op jit(solution)/shard_map/pallas_call | solution.py:113
  25.6 0.0 copy-done.2
  25.6 0.0 copy-done.6
  25.7 20.6 %shard_map.104 = (f32[4,16,2880]{2,1,0:T(8,128)S(1)}, f32[4,16,2880]{2,1,0:T(8,128)S(1)}, f32[4,16,2880]{2,1,0:T(8,128)S(1)}) custom-call(f32[3,4,16,2880]{3,2,1,0:T(8,128)S(1)} %shard_map.103.refs_0_, f32[4,16,2880]{2,1,0:T(8,128)S(1)} %copy-done.2, f32[256,3]{1,0:T(8,128)S(1)} %copy-done.6), custom_call_target="tpu_custom_call" | custom-call | tf_op jit(solution)/shard_map/pallas_call | solution.py:249
  46.3 0.9 %copy.15 = f32[4,16,2880]{2,1,0:T(8,128)} copy(f32[4,16,2880]{2,1,0:T(8,128)S(1)} %get-tuple-element.8) | data formatting | bytes 1474560
  47.1 0.9 %copy.16 = f32[4,16,2880]{2,1,0:T(8,128)} copy(f32[4,16,2880]{2,1,0:T(8,128)S(1)} %get-tuple-element.9) | data formatting | bytes 1474560
  48.0 0.9 %copy.17 = f32[4,16,2880]{2,1,0:T(8,128)} copy(f32[4,16,2880]{2,1,0:T(8,128)S(1)} %get-tuple-element.10) | data formatting | bytes 1474560
  (1 shorter events, 0.0 us)
Async XLA Ops:
  2.8 2.3 %copy-start = (bf16[6,1440,256]{2,1,0:T(8,128)(2,1)S(1)}, bf16[6,1440,256]{2,1,0:T(8,128)(2,1)}, u32[]{:S(2)}) copy-start(bf16[6,1440,256]{2,1,0:T(8,128)(2,1)} %constant.23.clone.refs_6_) | copy-start | bytes 13271044
  5.1 2.3 %copy-start.1 = (bf16[6,1440,256]{2,1,0:T(8,128)(2,1)S(1)}, bf16[6,1440,256]{2,1,0:T(8,128)(2,1)}, u32[]{:S(2)}) copy-start(bf16[6,1440,256]{2,1,0:T(8,128)(2,1)} %constant.22.clone.refs_5_) | copy-start | bytes 13271044
  7.3 1.1 %copy-start.3 = (f32[4,16,2880]{2,1,0:T(8,128)S(1)}, f32[4,16,2880]{2,1,0:T(8,128)}, u32[]{:S(2)}) copy-start(f32[4,16,2880]{2,1,0:T(8,128)} %refs_1_.2) | copy-start | bytes 2211844
  8.4 1.1 %copy-start.4 = (f32[4,16,2880]{2,1,0:T(8,128)S(1)}, f32[4,16,2880]{2,1,0:T(8,128)}, u32[]{:S(2)}) copy-start(f32[4,16,2880]{2,1,0:T(8,128)} %refs_2_.2) | copy-start | bytes 2211844
  9.5 1.1 %copy-start.5 = (f32[4,16,2880]{2,1,0:T(8,128)S(1)}, f32[4,16,2880]{2,1,0:T(8,128)}, u32[]{:S(2)}) copy-start(f32[4,16,2880]{2,1,0:T(8,128)} %refs_3_.1) | copy-start | bytes 2211844
  10.7 15.0 %copy-start.2 = (f32[4,16,2880]{2,1,0:T(8,128)S(1)}, f32[4,16,2880]{2,1,0:T(8,128)}, u32[]{:S(2)}) copy-start(f32[4,16,2880]{2,1,0:T(8,128)} %refs_1_.3) | copy-start | bytes 2211844
  10.7 15.0 %copy-start.6 = (f32[256,3]{1,0:T(8,128)S(1)}, f32[256,3]{1,0:T(8,128)}, u32[]{:S(2)}) copy-start(f32[256,3]{1,0:T(8,128)} %constant.24.clone.refs_2_) | copy-start | bytes 9220
where the time goes:
time: 49.2 us; the launch traced here: 48.9 us
  Pallas kernels  35.5 us (72%)
  local copies, waits for them, and re-layouts  10.6 us (22%)
  other arithmetic  1.39 us (3%)
  between operations  1.35 us (3%)
    pallas_call x1, Pallas kernels, advected(): pl.pallas_call(lambda *refs: advect_kernel(lat_count, lev_count, *refs),...  20.6 us
    pallas_call x1, Pallas kernels, filtered_fields(): pl.pallas_call(lambda *refs: filter_kernel(steps // 2, *refs), out_shape=...  15 us
    unnamed x17, local copies, waits for them, and re-layouts  10.5 us
    reduce_or x1, other arithmetic, filtered_fields(): flag = jnp.any(own_cut < HALF).astype(jnp.int32)[None]  1.39 us

commit v1 on v0

v1 whole, which is shorter than its diff:
```python
import math

import jax
import jax.numpy as jnp
import ml_dtypes
import numpy as np
from jax import lax
from jax.experimental import pallas as pl
from jax.experimental.pallas import tpu as pltpu
from jax.sharding import PartitionSpec as P

NLON = 2880
KMAX = 720
HALF = NLON // 2
CHUNK = 128
MESH = pl.DeviceIdType.MESH
QUARTER = 0.025


def half_tables():
    modes = KMAX // 2
    chunks = -(-modes // CHUNK)
    tables = np.zeros((2, chunks, HALF, 2 * CHUNK), np.float32)
    points = np.arange(HALF, dtype=np.int64)
    for parity in range(2):
        for chunk in range(chunks):
            ids = np.arange(chunk * CHUNK, min((chunk + 1) * CHUNK, modes), dtype=np.int64)
            angles = (points[:, None] * (2 * ids + parity)[None, :] % NLON) * (2.0 * math.pi / NLON)
            tables[parity, chunk, :, : len(ids)] = np.cos(angles)
            tables[parity, chunk, :, CHUNK : CHUNK + len(ids)] = np.sin(angles)
    tables = tables.reshape(2 * chunks, HALF, 2 * CHUNK)
    high = tables.astype(ml_dtypes.bfloat16)
    low = (tables - high.astype(np.float32)).astype(ml_dtypes.bfloat16)
    return high, low


def split(x):
    high = x.astype(jnp.bfloat16)
    return high, (x - high.astype(jnp.float32)).astype(jnp.bfloat16)


def dot(a, b, transposed=False):
    dims = (((1,), (1 if transposed else 0,)), ((), ()))
    return lax.dot_general(a, b, dims, preferred_element_type=jnp.float32)


def latitude_factors(total_rows):
    ids = np.arange(total_rows + 1, dtype=np.float64)
    face = np.sin(ids * (math.pi / total_rows))
    center = np.sin((ids[:-1] + 0.5) * (math.pi / total_rows))
    return np.stack(
        [QUARTER * face[:-1] / center, QUARTER * face[1:] / center, QUARTER / center], axis=1
    ).astype(np.float32)


def east_of(x):
    return jnp.concatenate([x[:, 1:], x[:, :1]], axis=1)


def west_of(x):
    return jnp.concatenate([x[:, -1:], x[:, :-1]], axis=1)


def kernel(
    lat_count, lev_count, cap, zonal_in, merid_in, tracer_in, wind_in, cut_ref, factor_ref, high_in, low_in,
    out0, out1, out2,
    field_ref, wind_ref, high_ref, low_ref, xh, xl, spec, spec_in, sh, sl, acc,
    lev_field, lev_wind, lat_out, lat_in,
    load_sem, table_sem, wind_send, wind_recv, raw_send, raw_recv, spec_send, spec_recv, lat_send, lat_recv,
):
    lat, lev = lax.axis_index("lat"), lax.axis_index("lev")
    inputs = (zonal_in, merid_in, tracer_in)
    outs = (out0, out1, out2)
    levels, lat_rows = wind_ref.shape[0], wind_ref.shape[1]
    steps = high_ref.shape[0]
    chunks = steps // 2
    edge = 3 * lat_rows
    rows = levels * edge
    half = lat_rows // 2
    total_rows = lat_count * lat_rows
    has = (lev > 0, lev < lev_count - 1, lat > 0, lat < lat_count - 1)
    there = ((lat, lev - 1), (lat, lev + 1), (lat - 1, lev), (lat + 1, lev))
    slots = 1 if lev_count == 2 else 2
    slot_of = (0, slots - 1)
    first_row = lat * lat_rows

    def spans(start, count):
        some = jnp.logical_or(start < cap, start + count > total_rows - cap)
        inside = jnp.logical_and(start + count > cap, start < total_rows - cap)
        return some, inside

    filtered, _ = spans(first_row, lat_rows)
    raw = tuple(spans(first_row + h * half, half)[1] for h in range(2))

    barrier = pltpu.get_barrier_semaphore()
    for side in range(4):
        @pl.when(has[side])
        def _():
            pl.semaphore_signal(barrier, inc=1, device_id=there[side], device_id_type=MESH)

    loads = [pltpu.make_async_copy(inputs[f], field_ref.at[f], load_sem.at[f]) for f in range(3)]
    load_wind = pltpu.make_async_copy(wind_in, wind_ref, load_sem.at[3])
    for copy in loads:
        copy.start()

    def table_loads(i):
        return (
            pltpu.make_async_copy(high_in.at[i], high_ref.at[i], table_sem.at[0, i]),
            pltpu.make_async_copy(low_in.at[i], low_ref.at[i], table_sem.at[1, i]),
        )

    @pl.when(filtered)
    def _():
        for i in range(steps):
            for copy in table_loads(i):
                copy.start()

    load_wind.start()
    pl.semaphore_wait(barrier, sum(side.astype(jnp.int32) for side in has))

    def remote(source, target, send, recv, to):
        return pltpu.make_async_remote_copy(
            src_ref=source, dst_ref=target, send_sem=send, recv_sem=recv,
            device_id=there[to], device_id_type=MESH,
        )

    edge_level = (0, levels - 1)

    def wind_copy(to):
        return remote(
            wind_in.at[edge_level[to]], lev_wind.at[1 - to], wind_send.at[to], wind_recv.at[1 - to], to
        )

    def raw_copy(to, f, h):
        span = pl.ds(h * half, half)
        return remote(
            inputs[f].at[edge_level[to], span], lev_field.at[1 - to, f, span],
            raw_send.at[to, f, h], raw_recv.at[1 - to, f, h], to,
        )

    def spec_copy(to, i):
        return remote(
            spec.at[i, pl.ds(edge_level[to] * edge, edge)], spec_in.at[1 - to, i],
            spec_send.at[to, i], spec_recv.at[1 - to, i], to,
        )

    def lat_copy(to):
        return remote(lat_out.at[to], lat_in.at[1 - to], lat_send.at[to], lat_recv.at[1 - to], 2 + to)

    for to in range(2):
        for h in range(2):
            @pl.when(jnp.logical_and(has[to], raw[h]))
            def _():
                for f in range(3):
                    raw_copy(to, f, h).start()

        @pl.when(jnp.logical_and(has[to], jnp.logical_not(filtered)))
        def _():
            wind_copy(to).start()

    for side in range(2):
        for h in range(2):
            @pl.when(jnp.logical_not(jnp.logical_and(has[side], raw[h])))
            def _():
                for f in range(3):
                    lev_field[side, f, pl.ds(h * half, half), :] = jnp.zeros((half, NLON), jnp.float32)

        @pl.when(jnp.logical_not(has[side]))
        def _():
            lev_wind[side] = jnp.zeros(lev_wind.shape[1:], jnp.float32)

        @pl.when(jnp.logical_not(has[2 + side]))
        def _():
            lat_in[side] = jnp.zeros(lat_in.shape[1:], jnp.float32)

    row = lax.broadcasted_iota(jnp.int32, (lat_rows, 1), 0)
    for copy in loads:
        copy.wait()

    @pl.when(filtered)
    def _():
        cut = jnp.zeros((lat_rows, 1), jnp.int32)
        for j in range(lat_rows):
            cut = jnp.where(row == j, cut_ref[first_row + j], cut)

        for l in range(levels):
            for f in range(3):
                x = field_ref[f, l]
                first, second = x[:, :HALF], x[:, HALF:]
                at = pl.ds(l * edge + f * lat_rows, lat_rows)
                for p, folded in enumerate((first + second, first - second)):
                    high, low = split(folded)
                    xh[p, at, :] = high
                    xl[p, at, :] = low

        def forward(i, carry):
            parity, chunk = i // chunks, i % chunks
            for copy in table_loads(i):
                copy.wait()
            th, tl = high_ref[i], low_ref[i]
            part = dot(xh[parity], th) + dot(xl[parity], th) + dot(xh[parity], tl)
            lane = lax.broadcasted_iota(jnp.int32, (lat_rows, 2 * CHUNK), 1) % CHUNK
            mode = 2 * (chunk * CHUNK + lane) + parity
            weight = jnp.where(mode == 0, jnp.float32(1.0 / NLON), jnp.float32(2.0 / NLON))
            weight = jnp.where(mode <= cut, weight, 0.0)
            part = part * jnp.concatenate([weight] * (3 * levels), axis=0)
            spec[i] = part
            for to in range(2):
                @pl.when(has[to])
                def _():
                    spec_copy(to, i).start()
            high, low = split(part)
            sh[i, pl.ds(0, rows), :] = high
            sl[i, pl.ds(0, rows), :] = low
            return carry

        lax.fori_loop(0, steps, forward, 0)
        for to in range(2):
            @pl.when(has[to])
            def _():
                wind_copy(to).start()

        def backward(i, carry):
            parity, chunk = i // chunks, i % chunks
            for side in range(2):
                at = pl.ds(rows + slot_of[side] * edge, edge)

                @pl.when(has[side])
                def _():
                    spec_copy(1 - side, i).wait_recv()
                    high, low = split(spec_in[side, i])
                    sh[i, at, :] = high
                    sl[i, at, :] = low

                if slots == 2:
                    @pl.when(jnp.logical_not(has[side]))
                    def _():
                        sh[i, at, :] = jnp.zeros((edge, 2 * CHUNK), jnp.bfloat16)
                        sl[i, at, :] = jnp.zeros((edge, 2 * CHUNK), jnp.bfloat16)

            th, tl = high_ref[i], low_ref[i]
            part = dot(sh[i], th, True) + dot(sl[i], th, True) + dot(sh[i], tl, True)

            @pl.when(chunk == 0)
            def _():
                acc[parity] = part

            @pl.when(chunk > 0)
            def _():
                acc[parity] += part

            return carry

        lax.fori_loop(0, steps, backward, 0)
        keep = cut < HALF

        def value(at):
            even, odd = acc[0, at, :], acc[1, at, :]
            return jnp.concatenate([even + odd, even - odd], axis=1)

        for l in range(levels):
            for f in range(3):
                y = value(pl.ds(l * edge + f * lat_rows, lat_rows))
                field_ref[f, l] = jnp.where(keep, y, field_ref[f, l])
        for side in range(2):
            for h in range(2):
                @pl.when(jnp.logical_and(has[side], raw[h]))
                def _():
                    for f in range(3):
                        raw_copy(1 - side, f, h).wait_recv()

            @pl.when(has[side])
            def _():
                for f in range(3):
                    y = value(pl.ds(rows + slot_of[side] * edge + f * lat_rows, lat_rows))
                    lev_field[side, f] = jnp.where(keep, y, lev_field[side, f])

    for to, at in ((0, 0), (1, lat_rows - 1)):
        for f in range(3):
            for l in range(levels):
                lat_out[to, f * levels + l : f * levels + l + 1, :] = field_ref[f, l, at : at + 1, :]

        @pl.when(has[2 + to])
        def _():
            lat_copy(to).start()

    load_wind.wait()
    factors = factor_ref[pl.ds(pl.multiple_of(first_row, lat_rows), lat_rows), :]
    low_face = jnp.where(row > 0, factors[:, 0:1], 0.0)
    high_face = jnp.where(row < lat_rows - 1, factors[:, 1:2], 0.0)
    zonal_factor = factors[:, 2:3]

    def inner(l, carry):
        below, above = jnp.maximum(l - 1, 0), jnp.minimum(l + 1, levels - 1)
        zonal = field_ref[0, l]
        merid = field_ref[1, l]
        wind_here = wind_ref[l]
        east_wind = (zonal + east_of(zonal)) * zonal_factor
        merid_pair = merid + jnp.roll(merid, 1, axis=0)
        low_wind = jnp.where(l > 0, jnp.float32(QUARTER), 0.0) * (wind_ref[below] + wind_here)
        high_wind = jnp.where(l < levels - 1, jnp.float32(QUARTER), 0.0) * (wind_here + wind_ref[above])
        for f in range(3):
            x = field_ref[f, l]
            flux_x = east_wind * (x + east_of(x))
            flux_y = merid_pair * (x + jnp.roll(x, 1, axis=0))
            div_y = high_face * jnp.roll(flux_y, -1, axis=0) - low_face * flux_y
            div_z = high_wind * (x + field_ref[f, above]) - low_wind * (field_ref[f, below] + x)
            outs[f][l] = x - (flux_x - west_of(flux_x)) - div_y - div_z
        return carry

    lax.fori_loop(0, levels, inner, 0)

    for side in range(2):
        @pl.when(has[2 + side])
        def _():
            lat_copy(1 - side).wait_recv()
    for side, at, factor in ((0, 0, factors[0:1, 0:1]), (1, lat_rows - 1, -factors[lat_rows - 1 :, 1:2])):
        for l in range(levels):
            own = pl.ds(at, 1)
            pair = factor * (lat_in[side, levels + l : levels + l + 1, :] + field_ref[1, l, own, :])
            for f in range(3):
                halo = lat_in[side, f * levels + l : f * levels + l + 1, :]
                outs[f][l, own, :] += pair * (halo + field_ref[f, l, own, :])

    for side in range(2):
        @pl.when(has[side])
        def _():
            wind_copy(1 - side).wait_recv()

        for h in range(2):
            @pl.when(jnp.logical_and(jnp.logical_and(has[side], raw[h]), jnp.logical_not(filtered)))
            def _():
                for f in range(3):
                    raw_copy(1 - side, f, h).wait_recv()
    for side, l, sign in ((0, 0, QUARTER), (1, levels - 1, -QUARTER)):
        pair = sign * (lev_wind[side] + wind_ref[l])
        for f in range(3):
            outs[f][l] += pair * (lev_field[side, f] + field_ref[f, l])
    for to in range(2):
        @pl.when(has[to])
        def _():
            wind_copy(to).wait_send()

        @pl.when(jnp.logical_and(has[to], filtered))
        def _():
            for i in range(steps):
                spec_copy(to, i).wait_send()

        for h in range(2):
            @pl.when(jnp.logical_and(has[to], raw[h]))
            def _():
                for f in range(3):
                    raw_copy(to, f, h).wait_send()

        @pl.when(has[2 + to])
        def _():
            lat_copy(to).wait_send()


def solution(mesh):
    lat_count, lev_count = mesh.shape["lat"], mesh.shape["lev"]

    def on_device(zonal_wind, merid_wind, tracer, vertical_wind, cutoff):
        levels, lat_rows, _ = zonal_wind.shape
        total_rows = lat_rows * lat_count
        cap = total_rows * 40 // 256
        high, low = half_tables()
        steps = high.shape[0]
        edge = 3 * lat_rows
        rows = levels * edge
        wide = rows + edge * (1 if lev_count == 2 else 2)
        vmem = pl.BlockSpec(memory_space=pltpu.VMEM)
        smem = pl.BlockSpec(memory_space=pltpu.SMEM)
        hbm = pl.BlockSpec(memory_space=pl.ANY)
        one = jax.ShapeDtypeStruct(zonal_wind.shape, jnp.float32)
        dma = pltpu.SemaphoreType.DMA
        return pl.pallas_call(
            lambda *refs: kernel(lat_count, lev_count, cap, *refs),
            out_shape=(one, one, one),
            in_specs=[hbm] * 4 + [smem, vmem, hbm, hbm],
            out_specs=(vmem,) * 3,
            scratch_shapes=[
                pltpu.VMEM((3, levels, lat_rows, NLON), jnp.float32),
                pltpu.VMEM((levels, lat_rows, NLON), jnp.float32),
                pltpu.VMEM(high.shape, jnp.bfloat16),
                pltpu.VMEM(low.shape, jnp.bfloat16),
                pltpu.VMEM((2, rows, HALF), jnp.bfloat16),
                pltpu.VMEM((2, rows, HALF), jnp.bfloat16),
                pltpu.VMEM((steps, rows, 2 * CHUNK), jnp.float32),
                pltpu.VMEM((2, steps, edge, 2 * CHUNK), jnp.float32),
                pltpu.VMEM((steps, wide, 2 * CHUNK), jnp.bfloat16),
                pltpu.VMEM((steps, wide, 2 * CHUNK), jnp.bfloat16),
                pltpu.VMEM((2, wide, HALF), jnp.float32),
                pltpu.VMEM((2, 3, lat_rows, NLON), jnp.float32),
                pltpu.VMEM((2, lat_rows, NLON), jnp.float32),
                pltpu.VMEM((2, 3 * levels, NLON), jnp.float32),
                pltpu.VMEM((2, 3 * levels, NLON), jnp.float32),
                dma((4,)), dma((2, steps)), dma((2,)), dma((2,)), dma((2, 3, 2)), dma((2, 3, 2)),
                dma((2, steps)), dma((2, steps)), dma((2,)), dma((2,)),
            ],
            compiler_params=pltpu.CompilerParams(
                collective_id=0, has_side_effects=True, vmem_limit_bytes=58 * 1024 * 1024
            ),
        )(
            zonal_wind, merid_wind, tracer, vertical_wind, cutoff,
            jnp.asarray(latitude_factors(total_rows)), jnp.asarray(high), jnp.asarray(low),
        )

    spec = P("lev", "lat", None)
    return jax.shard_map(
        on_device, mesh=mesh, in_specs=(spec,) * 4 + (P(),), out_specs=(spec,) * 3, check_vma=False
    )
```

time: 49.2 us -> 33.9 us (0.69)
  Pallas kernels: 35.5 us -> 26.8 us
  local copies, waits for them, and re-layouts: 10.6 us -> 6.12 us
  other arithmetic: 1.39 us -> 0 us
  between operations: 1.35 us -> 0.64 us
    pallas_call x2 -> x1, Pallas kernels: 35.5 us -> 26.8 us  [on_device(): pl.pallas_call(lambda *refs: kernel(lat_count, lev_count, cap, *refs), ou...]
    unnamed x17 -> x3, local copies, waits for them, and re-layouts: 10.5 us -> 6.12 us
    reduce_or x1 -> x0, other arithmetic: 1.39 us -> none  [filtered_fields(): flag = jnp.any(own_cut < HALF).astype(jnp.int32)[None]]
where the time goes in v1:
time: 33.9 us; the launch traced here: 33.6 us
  Pallas kernels  26.8 us (79%)
  local copies, waits for them, and re-layouts  6.12 us (18%)
  between operations  0.64 us (2%)
    pallas_call x1, Pallas kernels, on_device(): pl.pallas_call(lambda *refs: kernel(lat_count, lev_count, cap, *refs), ou...  26.8 us
    unnamed x3, local copies, waits for them, and re-layouts  6.12 us

profile of v1, /device:TPU:1, one launch (start us, length us, event | category | flops | bytes accessed | tf_op | source)
XLA Modules:
  0.0 33.6 jit_solution(3808111588464089753)
XLA Ops:
  0.6 26.8 %shard_map.103 = (f32[4,16,2880]{2,1,0:T(8,128)}, f32[4,16,2880]{2,1,0:T(8,128)}, f32[4,16,2880]{2,1,0:T(8,128)}) custom-call(f32[4,16,2880]{2,1,0:T(8,128)} %refs_0_.1, f32[4,16,2880]{2,1,0:T(8,128)} %refs_1_.1, f32[4,16,2880]{2,1,0:T(8,128)} %refs_2_.1, f32[4,16,2880]{2,1,0:T(8,128)} %refs_3_.1, s32[256]{0:T(256)} %refs_4_.1, ...), custom_call_target="tpu_custom_call" | custom-call | tf_op jit(solution)/shard_map/pallas_call | solution.py:377
  27.5 2.0 %copy.14 = f32[4,16,2880]{2,1,0:T(8,128)} copy(f32[4,16,2880]{2,1,0:T(8,128)} %get-tuple-element.6) | data formatting | bytes 1474560
  29.5 2.0 %copy.15 = f32[4,16,2880]{2,1,0:T(8,128)} copy(f32[4,16,2880]{2,1,0:T(8,128)} %get-tuple-element.7) | data formatting | bytes 1474560
  31.6 2.0 %copy.16 = f32[4,16,2880]{2,1,0:T(8,128)} copy(f32[4,16,2880]{2,1,0:T(8,128)} %get-tuple-element.8) | data formatting | bytes 1474560

commit v2 on v1

--- a/solution.py
+++ b/solution.py
@@ -177,11 +177,19 @@
     for copy in loads:
         copy.wait()
 
-    @pl.when(filtered)
-    def _():
+    def own_cut():
         cut = jnp.zeros((lat_rows, 1), jnp.int32)
         for j in range(lat_rows):
             cut = jnp.where(row == j, cut_ref[first_row + j], cut)
+        return cut
+
+    def value(at):
+        even, odd = acc[0, at, :], acc[1, at, :]
+        return jnp.concatenate([even + odd, even - odd], axis=1)
+
+    @pl.when(filtered)
+    def _():
+        cut = own_cut()
 
         for l in range(levels):
             for f in range(3):
@@ -254,26 +262,10 @@
         lax.fori_loop(0, steps, backward, 0)
         keep = cut < HALF
 
-        def value(at):
-            even, odd = acc[0, at, :], acc[1, at, :]
-            return jnp.concatenate([even + odd, even - odd], axis=1)
-
         for l in range(levels):
             for f in range(3):
                 y = value(pl.ds(l * edge + f * lat_rows, lat_rows))
                 field_ref[f, l] = jnp.where(keep, y, field_ref[f, l])
-        for side in range(2):
-            for h in range(2):
-                @pl.when(jnp.logical_and(has[side], raw[h]))
-                def _():
-                    for f in range(3):
-                        raw_copy(1 - side, f, h).wait_recv()
-
-            @pl.when(has[side])
-            def _():
-                for f in range(3):
-                    y = value(pl.ds(rows + slot_of[side] * edge + f * lat_rows, lat_rows))
-                    lev_field[side, f] = jnp.where(keep, y, lev_field[side, f])
 
     for to, at in ((0, 0), (1, lat_rows - 1)):
         for f in range(3):
@@ -328,10 +320,17 @@
             wind_copy(1 - side).wait_recv()
 
         for h in range(2):
-            @pl.when(jnp.logical_and(jnp.logical_and(has[side], raw[h]), jnp.logical_not(filtered)))
+            @pl.when(jnp.logical_and(has[side], raw[h]))
             def _():
                 for f in range(3):
                     raw_copy(1 - side, f, h).wait_recv()
+
+        @pl.when(jnp.logical_and(has[side], filtered))
+        def _():
+            keep = own_cut() < HALF
+            for f in range(3):
+                y = value(pl.ds(rows + slot_of[side] * edge + f * lat_rows, lat_rows))
+                lev_field[side, f] = jnp.where(keep, y, lev_field[side, f])
     for side, l, sign in ((0, 0, QUARTER), (1, levels - 1, -QUARTER)):
         pair = sign * (lev_wind[side] + wind_ref[l])
         for f in range(3):
@@ -355,6 +354,21 @@
         @pl.when(has[2 + to])
         def _():
             lat_copy(to).wait_send()
+
+
+def store_kernel(*refs):
+    for f in range(3):
+        refs[3 + f][...] = refs[f][...]
+
+
+def stored(fields):
+    levels, lat_rows, _ = fields[0].shape
+    block = pl.BlockSpec((1, lat_rows, NLON), lambda l: (l, 0, 0))
+    one = jax.ShapeDtypeStruct(fields[0].shape, jnp.float32)
+    return pl.pallas_call(
+        store_kernel, grid=(levels,), out_shape=(one,) * 3, in_specs=[block] * 3, out_specs=(block,) * 3,
+        compiler_params=pltpu.CompilerParams(vmem_limit_bytes=58 * 1024 * 1024),
+    )(*fields)
 
 
 def solution(mesh):
@@ -374,7 +388,7 @@
         hbm = pl.BlockSpec(memory_space=pl.ANY)
         one = jax.ShapeDtypeStruct(zonal_wind.shape, jnp.float32)
         dma = pltpu.SemaphoreType.DMA
-        return pl.pallas_call(
+        fields = pl.pallas_call(
             lambda *refs: kernel(lat_count, lev_count, cap, *refs),
             out_shape=(one, one, one),
             in_specs=[hbm] * 4 + [smem, vmem, hbm, hbm],
@@ -405,6 +419,7 @@
             zonal_wind, merid_wind, tracer, vertical_wind, cutoff,
             jnp.asarray(latitude_factors(total_rows)), jnp.asarray(high), jnp.asarray(low),
         )
+        return stored(fields)
 
     spec = P("lev", "lat", None)
     return jax.shard_map(

time: 33.9 us -> 31.6 us (0.932)
  local copies, waits for them, and re-layouts: 6.12 us -> 0 us
  Pallas kernels: 26.8 us -> 30.7 us
    unnamed x3 -> x0, local copies, waits for them, and re-layouts: 6.12 us -> none
    pallas_call x0 -> x1, Pallas kernels: none -> 3.87 us  [stored(): pl.pallas_call(store_kernel, grid=(levels,), out_shape=(one,) * 3, in_spe...]
where the time goes in v2:
time: 31.6 us; the launch traced here: 31.3 us
  Pallas kernels  30.7 us (97%)
  between operations  0.64 us (2%)
    pallas_call x1, Pallas kernels, on_device(): pl.pallas_call(lambda *refs: kernel(lat_count, lev_count, cap, *refs), ou...  26.8 us
    pallas_call x1, Pallas kernels, stored(): pl.pallas_call(store_kernel, grid=(levels,), out_shape=(one,) * 3, in_spe...  3.87 us

profile of v2, /device:TPU:1, one launch (start us, length us, event | category | flops | bytes accessed | tf_op | source)
XLA Modules:
  0.0 31.3 jit_solution(1988188414222014371)
XLA Ops:
  0.6 26.8 %shard_map.103 = (f32[4,16,2880]{2,1,0:T(8,128)}, f32[4,16,2880]{2,1,0:T(8,128)}, f32[4,16,2880]{2,1,0:T(8,128)}) custom-call(f32[4,16,2880]{2,1,0:T(8,128)} %refs_0_.1, f32[4,16,2880]{2,1,0:T(8,128)} %refs_1_.1, f32[4,16,2880]{2,1,0:T(8,128)} %refs_2_.1, f32[4,16,2880]{2,1,0:T(8,128)} %refs_3_.1, s32[256]{0:T(256)} %refs_4_.1, ...), custom_call_target="tpu_custom_call" | custom-call | tf_op jit(solution)/shard_map/pallas_call | solution.py:391
  27.5 3.9 %shard_map.104 = (f32[4,16,2880]{2,1,0:T(8,128)}, f32[4,16,2880]{2,1,0:T(8,128)}, f32[4,16,2880]{2,1,0:T(8,128)}) custom-call(f32[4,16,2880]{2,1,0:T(8,128)} %get-tuple-element.6.refs_0_, f32[4,16,2880]{2,1,0:T(8,128)} %get-tuple-element.7.refs_1_, f32[4,16,2880]{2,1,0:T(8,128)} %get-tuple-element.8.refs_2_), custom_call_target="tpu_custom_call" | custom-call | tf_op jit(solution)/shard_map/pallas_call | solution.py:368

commit v3 on v2

--- a/solution.py
+++ b/solution.py
@@ -65,12 +65,13 @@
     lat_count, lev_count, cap, zonal_in, merid_in, tracer_in, wind_in, cut_ref, factor_ref, high_in, low_in,
     out0, out1, out2,
     field_ref, wind_ref, high_ref, low_ref, xh, xl, spec, spec_in, sh, sl, acc,
-    lev_field, lev_wind, lat_out, lat_in,
-    load_sem, table_sem, wind_send, wind_recv, raw_send, raw_recv, spec_send, spec_recv, lat_send, lat_recv,
+    lev_field, lev_wind, lat_out, lat_in, out_ref,
+    load_sem, out_sem, table_sem, wind_send, wind_recv, raw_send, raw_recv, spec_send, spec_recv, lat_send, lat_recv,
 ):
     lat, lev = lax.axis_index("lat"), lax.axis_index("lev")
     inputs = (zonal_in, merid_in, tracer_in)
-    outs = (out0, out1, out2)
+    results = (out0, out1, out2)
+    outs = (out_ref.at[0], out_ref.at[1], out_ref.at[2])
     levels, lat_rows = wind_ref.shape[0], wind_ref.shape[1]
     steps = high_ref.shape[0]
     chunks = steps // 2
@@ -90,7 +91,13 @@
         return some, inside
 
     filtered, _ = spans(first_row, lat_rows)
-    raw = tuple(spans(first_row + h * half, half)[1] for h in range(2))
+    mixed = jnp.logical_and(filtered, spans(first_row, lat_rows)[1])
+    pure = jnp.logical_and(filtered, jnp.logical_not(mixed))
+    early = tuple(jnp.logical_not(spans(first_row + h * half, half)[0]) for h in range(2))
+    late = tuple(jnp.logical_and(mixed, jnp.logical_not(early[h])) for h in range(2))
+
+    def result_copy(f, l):
+        return pltpu.make_async_copy(out_ref.at[f, l], results[f].at[l], out_sem.at[f, l])
 
     barrier = pltpu.get_barrier_semaphore()
     for side in range(4):
@@ -131,10 +138,10 @@
             wind_in.at[edge_level[to]], lev_wind.at[1 - to], wind_send.at[to], wind_recv.at[1 - to], to
         )
 
-    def raw_copy(to, f, h):
+    def raw_copy(to, f, h, source=inputs):
         span = pl.ds(h * half, half)
         return remote(
-            inputs[f].at[edge_level[to], span], lev_field.at[1 - to, f, span],
+            source[f].at[edge_level[to], span], lev_field.at[1 - to, f, span],
             raw_send.at[to, f, h], raw_recv.at[1 - to, f, h], to,
         )
 
@@ -149,21 +156,19 @@
 
     for to in range(2):
         for h in range(2):
-            @pl.when(jnp.logical_and(has[to], raw[h]))
+            @pl.when(jnp.logical_and(has[to], early[h]))
             def _():
                 for f in range(3):
                     raw_copy(to, f, h).start()
 
-        @pl.when(jnp.logical_and(has[to], jnp.logical_not(filtered)))
+        @pl.when(jnp.logical_and(has[to], jnp.logical_not(pure)))
         def _():
             wind_copy(to).start()
 
     for side in range(2):
-        for h in range(2):
-            @pl.when(jnp.logical_not(jnp.logical_and(has[side], raw[h])))
-            def _():
-                for f in range(3):
-                    lev_field[side, f, pl.ds(h * half, half), :] = jnp.zeros((half, NLON), jnp.float32)
+        @pl.when(jnp.logical_or(jnp.logical_not(has[side]), pure))
+        def _():
+            lev_field[side] = jnp.zeros(lev_field.shape[1:], jnp.float32)
 
         @pl.when(jnp.logical_not(has[side]))
         def _():
@@ -214,7 +219,7 @@
             part = part * jnp.concatenate([weight] * (3 * levels), axis=0)
             spec[i] = part
             for to in range(2):
-                @pl.when(has[to])
+                @pl.when(jnp.logical_and(has[to], pure))
                 def _():
                     spec_copy(to, i).start()
             high, low = split(part)
@@ -224,7 +229,7 @@
 
         lax.fori_loop(0, steps, forward, 0)
         for to in range(2):
-            @pl.when(has[to])
+            @pl.when(jnp.logical_and(has[to], pure))
             def _():
                 wind_copy(to).start()
 
@@ -233,18 +238,19 @@
             for side in range(2):
                 at = pl.ds(rows + slot_of[side] * edge, edge)
 
-                @pl.when(has[side])
+                @pl.when(jnp.logical_and(has[side], pure))
                 def _():
                     spec_copy(1 - side, i).wait_recv()
                     high, low = split(spec_in[side, i])
                     sh[i, at, :] = high
                     sl[i, at, :] = low
 
-                if slots == 2:
-                    @pl.when(jnp.logical_not(has[side]))
-                    def _():
-                        sh[i, at, :] = jnp.zeros((edge, 2 * CHUNK), jnp.bfloat16)
-                        sl[i, at, :] = jnp.zeros((edge, 2 * CHUNK), jnp.bfloat16)
+                empty = jnp.logical_not(jnp.logical_and(has[side], pure)) if slots == 2 else mixed
+
+                @pl.when(empty)
+                def _():
+                    sh[i, at, :] = jnp.zeros((edge, 2 * CHUNK), jnp.bfloat16)
+                    sl[i, at, :] = jnp.zeros((edge, 2 * CHUNK), jnp.bfloat16)
 
             th, tl = high_ref[i], low_ref[i]
             part = dot(sh[i], th, True) + dot(sl[i], th, True) + dot(sh[i], tl, True)
@@ -266,6 +272,13 @@
             for f in range(3):
                 y = value(pl.ds(l * edge + f * lat_rows, lat_rows))
                 field_ref[f, l] = jnp.where(keep, y, field_ref[f, l])
+
+    for to in range(2):
+        for h in range(2):
+            @pl.when(jnp.logical_and(has[to], late[h]))
+            def _():
+                for f in range(3):
+                    raw_copy(to, f, h, (field_ref.at[0], field_ref.at[1], field_ref.at[2])).start()
 
     for to, at in ((0, 0), (1, lat_rows - 1)):
         for f in range(3):
@@ -313,6 +326,9 @@
             for f in range(3):
                 halo = lat_in[side, f * levels + l : f * levels + l + 1, :]
                 outs[f][l, own, :] += pair * (halo + field_ref[f, l, own, :])
+    for l in range(1, levels - 1):
+        for f in range(3):
+            result_copy(f, l).start()
 
     for side in range(2):
         @pl.when(has[side])
@@ -320,12 +336,12 @@
             wind_copy(1 - side).wait_recv()
 
         for h in range(2):
-            @pl.when(jnp.logical_and(has[side], raw[h]))
+            @pl.when(jnp.logical_and(has[side], jnp.logical_not(pure)))
             def _():
                 for f in range(3):
                     raw_copy(1 - side, f, h).wait_recv()
 
-        @pl.when(jnp.logical_and(has[side], filtered))
+        @pl.when(jnp.logical_and(has[side], pure))
         def _():
             keep = own_cut() < HALF
             for f in range(3):
@@ -335,18 +351,22 @@
         pair = sign * (lev_wind[side] + wind_ref[l])
         for f in range(3):
             outs[f][l] += pair * (lev_field[side, f] + field_ref[f, l])
+            result_copy(f, l).start()
+    for l in range(levels):
+        for f in range(3):
+            result_copy(f, l).wait()
     for to in range(2):
         @pl.when(has[to])
         def _():
             wind_copy(to).wait_send()
 
-        @pl.when(jnp.logical_and(has[to], filtered))
+        @pl.when(jnp.logical_and(has[to], pure))
         def _():
             for i in range(steps):
                 spec_copy(to, i).wait_send()
 
         for h in range(2):
-            @pl.when(jnp.logical_and(has[to], raw[h]))
+            @pl.when(jnp.logical_and(has[to], jnp.logical_not(pure)))
             def _():
                 for f in range(3):
                     raw_copy(to, f, h).wait_send()
@@ -356,17 +376,28 @@
             lat_copy(to).wait_send()
 
 
-def store_kernel(*refs):
-    for f in range(3):
-        refs[3 + f][...] = refs[f][...]
+def store_kernel(in0, in1, in2, out0, out1, out2, held, in_sem, out_sem):
+    sources, results = (in0, in1, in2), (out0, out1, out2)
+    parts = [(f, l) for l in range(in0.shape[0]) for f in range(3)]
+    reads = [pltpu.make_async_copy(sources[f].at[l], held.at[f, l], in_sem.at[f, l]) for f, l in parts]
+    writes = [pltpu.make_async_copy(held.at[f, l], results[f].at[l], out_sem.at[f, l]) for f, l in parts]
+    for copy in reads:
+        copy.start()
+    for read, write in zip(reads, writes):
+        read.wait()
+        write.start()
+    for copy in writes:
+        copy.wait()
 
 
 def stored(fields):
-    levels, lat_rows, _ = fields[0].shape
-    block = pl.BlockSpec((1, lat_rows, NLON), lambda l: (l, 0, 0))
-    one = jax.ShapeDtypeStruct(fields[0].shape, jnp.float32)
+    shape = fields[0].shape
+    hbm = pl.BlockSpec(memory_space=pl.ANY)
+    one = jax.ShapeDtypeStruct(shape, jnp.float32)
+    dma = pltpu.SemaphoreType.DMA
     return pl.pallas_call(
-        store_kernel, grid=(levels,), out_shape=(one,) * 3, in_specs=[block] * 3, out_specs=(block,) * 3,
+        store_kernel, out_shape=(one,) * 3, in_specs=[hbm] * 3, out_specs=(hbm,) * 3,
+        scratch_shapes=[pltpu.VMEM((3,) + shape, jnp.float32), dma((3, shape[0])), dma((3, shape[0]))],
         compiler_params=pltpu.CompilerParams(vmem_limit_bytes=58 * 1024 * 1024),
     )(*fields)
 
@@ -392,7 +423,7 @@
             lambda *refs: kernel(lat_count, lev_count, cap, *refs),
             out_shape=(one, one, one),
             in_specs=[hbm] * 4 + [smem, vmem, hbm, hbm],
-            out_specs=(vmem,) * 3,
+            out_specs=(hbm,) * 3,
             scratch_shapes=[
                 pltpu.VMEM((3, levels, lat_rows, NLON), jnp.float32),
                 pltpu.VMEM((levels, lat_rows, NLON), jnp.float32),
@@ -409,7 +440,8 @@
                 pltpu.VMEM((2, lat_rows, NLON), jnp.float32),
                 pltpu.VMEM((2, 3 * levels, NLON), jnp.float32),
                 pltpu.VMEM((2, 3 * levels, NLON), jnp.float32),
-                dma((4,)), dma((2, steps)), dma((2,)), dma((2,)), dma((2, 3, 2)), dma((2, 3, 2)),
+                pltpu.VMEM((3, levels, lat_rows, NLON), jnp.float32),
+                dma((4,)), dma((3, levels)), dma((2, steps)), dma((2,)), dma((2,)), dma((2, 3, 2)), dma((2, 3, 2)),
                 dma((2, steps)), dma((2, steps)), dma((2,)), dma((2,)),
             ],
             compiler_params=pltpu.CompilerParams(

time: 31.6 us -> 27.7 us (0.88)
  the two profiles are of different devices: /device:TPU:1 before, /device:TPU:25 now
where the time goes in v3:
time: 27.7 us; the launch traced here: 27.6 us
  Pallas kernels  26.9 us (97%)
  between operations  0.64 us (2%)
    pallas_call x1, Pallas kernels, on_device(): pl.pallas_call(lambda *refs: kernel(lat_count, lev_count, cap, *refs), ou...  24.4 us
    pallas_call x1, Pallas kernels, stored(): pl.pallas_call(store_kernel, out_shape=(one,) * 3, in_specs=[hbm] * 3, ou...  2.58 us

profile of v3, /device:TPU:25, one launch (start us, length us, event | category | flops | bytes accessed | tf_op | source)
XLA Modules:
  0.0 27.6 jit_solution(15058052122371915622)
XLA Ops:
  0.6 24.4 %shard_map.103 = (f32[4,16,2880]{2,1,0:T(8,128)}, f32[4,16,2880]{2,1,0:T(8,128)}, f32[4,16,2880]{2,1,0:T(8,128)}) custom-call(f32[4,16,2880]{2,1,0:T(8,128)} %refs_0_.1, f32[4,16,2880]{2,1,0:T(8,128)} %refs_1_.1, f32[4,16,2880]{2,1,0:T(8,128)} %refs_2_.1, f32[4,16,2880]{2,1,0:T(8,128)} %refs_3_.1, s32[256]{0:T(256)} %refs_4_.1, ...), custom_call_target="tpu_custom_call" | custom-call | tf_op jit(solution)/shard_map/pallas_call | solution.py:422
  25.0 2.6 %shard_map.104 = (f32[4,16,2880]{2,1,0:T(8,128)}, f32[4,16,2880]{2,1,0:T(8,128)}, f32[4,16,2880]{2,1,0:T(8,128)}) custom-call(f32[4,16,2880]{2,1,0:T(8,128)} %get-tuple-element.6.in0, f32[4,16,2880]{2,1,0:T(8,128)} %get-tuple-element.7.in1, f32[4,16,2880]{2,1,0:T(8,128)} %get-tuple-element.8.in2), custom_call_target="tpu_custom_call" | custom-call | tf_op jit(solution)/shard_map/pallas_call | solution.py:398

commit v4 on v3

--- a/solution.py
+++ b/solution.py
@@ -253,15 +253,27 @@
                     sl[i, at, :] = jnp.zeros((edge, 2 * CHUNK), jnp.bfloat16)
 
             th, tl = high_ref[i], low_ref[i]
-            part = dot(sh[i], th, True) + dot(sl[i], th, True) + dot(sh[i], tl, True)
-
-            @pl.when(chunk == 0)
-            def _():
-                acc[parity] = part
-
-            @pl.when(chunk > 0)
-            def _():
-                acc[parity] += part
+
+            def inverse(count):
+                at = pl.ds(0, count)
+                high, low = sh[i, at, :], sl[i, at, :]
+                part = dot(high, th, True) + dot(low, th, True) + dot(high, tl, True)
+
+                @pl.when(chunk == 0)
+                def _():
+                    acc[parity, at, :] = part
+
+                @pl.when(chunk > 0)
+                def _():
+                    acc[parity, at, :] += part
+
+            @pl.when(pure)
+            def _():
+                inverse(sh.shape[1])
+
+            @pl.when(mixed)
+            def _():
+                inverse(rows)
 
             return carry
 

time: 27.7 us -> 27.9 us (level)
  the two profiles are of different devices: /device:TPU:25 before, /device:TPU:1 now
where the time goes in v4:
time: 27.9 us; the launch traced here: 27.6 us
  Pallas kernels  27 us (97%)
  between operations  0.64 us (2%)
    pallas_call x1, Pallas kernels, on_device(): pl.pallas_call(lambda *refs: kernel(lat_count, lev_count, cap, *refs), ou...  24.4 us
    pallas_call x1, Pallas kernels, stored(): pl.pallas_call(store_kernel, out_shape=(one,) * 3, in_specs=[hbm] * 3, ou...  2.58 us

profile of v4, /device:TPU:1, one launch (start us, length us, event | category | flops | bytes accessed | tf_op | source)
XLA Modules:
  0.0 27.6 jit_solution(5377680479229741817)
XLA Ops:
  0.6 24.4 %shard_map.103 = (f32[4,16,2880]{2,1,0:T(8,128)}, f32[4,16,2880]{2,1,0:T(8,128)}, f32[4,16,2880]{2,1,0:T(8,128)}) custom-call(f32[4,16,2880]{2,1,0:T(8,128)} %refs_0_.1, f32[4,16,2880]{2,1,0:T(8,128)} %refs_1_.1, f32[4,16,2880]{2,1,0:T(8,128)} %refs_2_.1, f32[4,16,2880]{2,1,0:T(8,128)} %refs_3_.1, s32[256]{0:T(256)} %refs_4_.1, ...), custom_call_target="tpu_custom_call" | custom-call | tf_op jit(solution)/shard_map/pallas_call | solution.py:434
  25.0 2.6 %shard_map.104 = (f32[4,16,2880]{2,1,0:T(8,128)}, f32[4,16,2880]{2,1,0:T(8,128)}, f32[4,16,2880]{2,1,0:T(8,128)}) custom-call(f32[4,16,2880]{2,1,0:T(8,128)} %get-tuple-element.6.in0, f32[4,16,2880]{2,1,0:T(8,128)} %get-tuple-element.7.in1, f32[4,16,2880]{2,1,0:T(8,128)} %get-tuple-element.8.in2), custom_call_target="tpu_custom_call" | custom-call | tf_op jit(solution)/shard_map/pallas_call | solution.py:410
